TPU v7x, 32 devices: a whole 2x2x4 slice. The times are simulated.
32 devices in a mesh: gz: 8 (over z, y), ky: 4 (over x, core).
Axes of the slice: x: 2, y: 2, z: 4, core: 2. Of those that a mesh axis runs over, the one named last changes fastest.
Arguments:
- fields: bfloat16 [256, 3, 2, 32768], P('gz', None, None, 'ky'), may hold values from -6 to 6
- wall_operator: bfloat16 [256, 256], replicated, may hold values from -0.375 to 0.375
- remap_offset: int32 [4, 4], replicated, may hold values from 0 to 31, as said below
- remap_count: int32 [4, 4], replicated, may hold values from 1 to 8, as said below
Outputs:
- spectra: float32 [256, 3, 2, 32768], P('gz', None, None, 'ky')
Inputs may be any that keep to these rules, and one draw needn't show every extreme that they name: remap_count[g, h] rows go from group g to group h; in every draw one group h receives exactly 8 rows from every group. The run from group g to group h is rows remap_offset[g, h] to remap_offset[g, h] + remap_count[g, h] - 1 of group g's 32 rows; the runs of one group do not intersect.
All inputs are finite; a program needn't handle non-finite values.
Results may differ from a plain program's by a relative error of at most 0.0048.
Values may be sent and summed in bfloat16 or wider, within the bound.
No kernel may reach another device: no remote copies, remote signals or barrier semaphores. Data moves between devices by JAX's collectives and lax.ppermute only.
A program may use at most 128 MiB of HBM per device.

v0:
```python
import math

import jax
import jax.numpy as jnp
from jax import lax
from jax.sharding import PartitionSpec as P

NU_COEF = 0.05
STEP_DT = 0.3


def mode_tables(half_z):
    row_index = jnp.arange(half_z, dtype=jnp.int32)[:, None]
    column_index = jnp.arange(half_z, dtype=jnp.int32)[None, :]
    norm_factor = math.sqrt(2.0 / half_z)
    angle_step = math.pi / (2 * half_z)
    cos_index = row_index * (2 * column_index + 1) % (4 * half_z)
    sin_index = (row_index + 1) * (2 * (half_z - 1 - column_index) + 1) % (4 * half_z)
    cos_table = (norm_factor * jnp.cos(cos_index.astype(jnp.float32) * angle_step)).astype(
        jnp.bfloat16
    )
    sin_table = (norm_factor * jnp.sin(sin_index.astype(jnp.float32) * angle_step)).astype(
        jnp.bfloat16
    )
    return (cos_table, sin_table)


def couple(mode_values, half_z):
    total_z = mode_values.shape[0]
    mode_index = jnp.arange(total_z, dtype=jnp.int32)
    wave_index = jnp.where(mode_index < half_z, mode_index, mode_index - half_z + 1)
    wave_number = wave_index.astype(jnp.float32) * (math.pi / half_z)
    wave_number = wave_number.reshape((total_z,) + (1,) * (mode_values.ndim - 2))
    damping = jnp.exp(-NU_COEF * wave_number * wave_number)
    velocity = mode_values[:, 0]
    buoyant = mode_values[:, 1]
    magnetic = mode_values[:, 2]
    new_velocity = damping * (velocity + STEP_DT * buoyant + STEP_DT * wave_number * magnetic)
    new_buoyant = damping * (buoyant - STEP_DT * velocity)
    new_magnetic = damping * (magnetic - STEP_DT * wave_number * velocity)
    return jnp.stack([new_velocity, new_buoyant, new_magnetic], axis=1)


def remap_index(offsets, counts, row_stride, rows_out):
    start_rows = jnp.cumsum(counts) - counts
    position = jnp.arange(rows_out, dtype=jnp.int32)
    inside = (position[None, :] >= start_rows[:, None]) & (
        position[None, :] < (start_rows + counts)[:, None]
    )
    group_index = jnp.arange(counts.shape[0], dtype=jnp.int32)
    source = (
        group_index[:, None] * row_stride
        + offsets[:, None]
        + position[None, :]
        - start_rows[:, None]
    )
    chosen = jnp.sum(jnp.where(inside, source, 0), axis=0)
    is_valid = jnp.any(inside, axis=0)
    return (chosen, is_valid)


def per_device(fields, wall_operator, remap_offset, remap_count):
    groups = lax.axis_size("ky")
    receiver = lax.axis_index("ky")
    local_z = fields.shape[0]
    width_x = wall_operator.shape[0]
    rows_dev = fields.shape[3] // width_x
    everything = lax.all_gather(fields, "ky", axis=3, tiled=True)
    source_rows = everything.reshape(local_z, 3, 2, groups * rows_dev, width_x)
    chosen, is_valid = remap_index(
        remap_offset[:, receiver], remap_count[:, receiver], rows_dev, rows_dev
    )
    remapped = jnp.take(source_rows, chosen, axis=3)
    remapped = jnp.where(is_valid[None, None, None, :, None], remapped, jnp.zeros((), jnp.bfloat16))
    walled = jnp.einsum(
        "zfcrx,xy->zfcry", remapped, wall_operator, preferred_element_type=jnp.float32
    ).astype(jnp.bfloat16)
    walled = walled.reshape(local_z, 3, 2, rows_dev * width_x)
    total_z = local_z * lax.axis_size("gz")
    half_z = total_z // 2
    cos_table, sin_table = mode_tables(half_z)
    pencil = lax.all_to_all(walled, "gz", split_axis=3, concat_axis=0, tiled=True)
    flipped = pencil[::-1]
    even_part = 0.5 * (pencil[:half_z].astype(jnp.float32) + flipped[:half_z].astype(jnp.float32))
    odd_part = 0.5 * (flipped[half_z:].astype(jnp.float32) - pencil[half_z:].astype(jnp.float32))
    parity = jnp.concatenate([even_part, odd_part]).astype(jnp.bfloat16)
    flat_parity = parity.reshape(total_z, -1)
    cosine = jnp.dot(cos_table, flat_parity[:half_z], preferred_element_type=jnp.float32)
    sine_part = jnp.dot(sin_table, flat_parity[half_z:], preferred_element_type=jnp.float32)
    mode_values = jnp.concatenate([cosine, sine_part]).reshape(parity.shape)
    coupled = couple(mode_values, half_z)
    return lax.all_to_all(coupled, "gz", split_axis=0, concat_axis=3, tiled=True)


def solution(mesh):
    placed = (P("gz", None, None, "ky"), P(), P(), P())
    return jax.shard_map(
        per_device, mesh=mesh, in_specs=placed, out_specs=P("gz", None, None, "ky"), check_vma=False
    )
```

profile of v0, /device:TPU:17, one launch (start us, length us, event | category | flops | bytes accessed | tf_op | source)
XLA Modules:
  0.0 501.3 jit_solution(5964029869696971043)
XLA Ops:
  6.5 0.7 all-gather.2.cloned.1.call-update
  7.9 84.7 %all-gather.2.cloned.1.call-done = bf16[32,3,2,32768]{3,2,1,0:T(2,128)(2,1)} async-done(((bf16[32,3,2,8192]{3,2,1,0:T(2,128)(2,1)}), bf16[32,3,2,32768]{3,2,1,0:T(2,128)(2,1)}) %all-gather.2.cloned.1.call-update) | async-done | bytes 12582928 | tf_op jit(solution)/shard_map/all_gather | solution.py:68
  92.6 20.5 %reshape.101 = bf16[32,3,2,128,256]{4,3,2,1,0:T(8,128)(2,1)} reshape(bf16[32,3,2,32768]{3,2,1,0:T(2,128)(2,1)} %all-gather.2.cloned.1.call-done) | data formatting | bytes 25165824 | tf_op jit(solution)/shard_map/reshape | solution.py:69
  113.0 14.0 %copy.62 = bf16[32,3,2,128,256]{4,0,3,2,1:T(8,128)(2,1)} copy(bf16[32,3,2,128,256]{4,3,2,1,0:T(8,128)(2,1)} %reshape.101) | data formatting | bytes 25165824 | tf_op jit(solution)/shard_map/reshape | solution.py:69
  127.0 5.3 %gather_fusion = bf16[32,32,3,2,256]{4,1,3,2,0:T(8,128)(2,1)S(1)} fusion(bf16[32,3,2,128,256]{4,0,3,2,1:T(8,128)(2,1)} %copy.62, s32[1024]{0:T(1024)S(1)} %pad_clamp_fusion), kind=kCustom, calls=%fused_computation | custom fusion | bytes 6291584 | tf_op jit(solution)/shard_map/jit(_take)/gather | solution.py:73
  132.8 3.6 fusion.2
  136.3 14.6 %copy.79 = bf16[32,3,2,32,256]{0,2,1,4,3:T(2,128)(2,1)} copy(bf16[32,3,2,32,256]{4,3,2,1,0:T(8,128)(2,1)S(1)} %fusion.2) | data formatting | bytes 6291456 | tf_op jit(solution)/shard_map/reshape | solution.py:78
  150.9 14.5 %reshape.105 = bf16[8,2,98304]{2,1,0:T(2,128)(2,1)} reshape(bf16[8192,3,2,32]{3,2,1,0:T(2,128)(2,1)} %bitcast.30) | data formatting | bytes 6291456
  165.4 5.5 %all-to-all-start = ((bf16[8,2,98304]{2,1,0:T(2,128)(2,1)}), bf16[8,2,98304]{2,1,0:T(2,128)(2,1)S(1)}, u32[]{:S(2)}, u32[]{:S(2)}) async-start(bf16[8,2,98304]{2,1,0:T(2,128)(2,1)} %reshape.105), calls=%async_computation | async-start | bytes 6291456 | tf_op jit(solution)/shard_map/all_to_all | solution.py:82
  170.9 67.3 %all-to-all-done = bf16[8,2,98304]{2,1,0:T(2,128)(2,1)S(1)} async-done(((bf16[8,2,98304]{2,1,0:T(2,128)(2,1)}), bf16[8,2,98304]{2,1,0:T(2,128)(2,1)S(1)}, u32[]{:S(2)}, u32[]{:S(2)}) %all-to-all-start) | async-done | bytes 3145760 | tf_op jit(solution)/shard_map/all_to_all | solution.py:82
  238.2 8.5 %reshape.106 = bf16[8192,3,2,32]{3,2,1,0:T(2,128)(2,1)} reshape(bf16[8,2,98304]{2,1,0:T(2,128)(2,1)S(1)} %all-to-all-done) | data formatting | bytes 6291456
  246.6 17.7 %copy.80 = bf16[32,3,2,8,1024]{4,3,0,2,1:T(8,128)(2,1)S(1)} copy(bf16[32,3,2,8,1024]{0,2,1,4,3:T(2,128)(2,1)} %bitcast.31) | data formatting | bytes 6291456 | tf_op jit(solution)/shard_map/all_to_all | solution.py:82
  264.3 2.3 fusion.55
  267.2 15.4 %slice.50 = bf16[128,3,2,1024]{3,0,2,1:T(8,128)(2,1)} reverse(bf16[128,3,2,1024]{3,0,2,1:T(8,128)(2,1)S(1)} %bitcast.34), dimensions={0} | reverse | bytes 3145728 | tf_op jit(solution)/shard_map/slice | solution.py:85
  282.5 2.0 copy.67
  284.6 2.0 multiply_convert_fusion
  286.5 2.6 copy.69
  289.1 15.3 %slice.47 = bf16[128,3,2,1024]{3,0,2,1:T(8,128)(2,1)} reverse(bf16[128,3,2,1024]{3,0,2,1:T(8,128)(2,1)S(1)} %bitcast.35), dimensions={0} | reverse | bytes 3145728 | tf_op jit(solution)/shard_map/slice | solution.py:84
  304.5 2.1 multiply_convert_fusion.1
  306.6 0.9 copy.68
  307.5 0.8 fusion.21
  308.9 0.9 fusion.23
  309.8 3.1 pad_maximum_fusion
  312.9 6.6 %copy.70 = f32[256,6144]{0,1:T(8,128)} copy(f32[256,6144]{1,0:T(8,128)} %pad_maximum_fusion) | data formatting | bytes 12582912 | tf_op jit(solution)/shard_map/concatenate | solution.py:90
  319.5 5.8 %fusion.54 = (f32[256,1,2,1024]{0,3,2,1:T(8,128)}, f32[256,1,2,1024]{0,3,2,1:T(8,128)}, f32[256,1,2,1024]{0,3,2,1:T(8,128)}) fusion(f32[256,3,2,1024]{0,3,2,1:T(8,128)} %bitcast.32), kind=kLoop, calls=%fused_computation.82 | loop fusion | bytes 12582912 | tf_op jit(solution)/shard_map/slice | solution.py:36
  325.3 1.9 copy.83
  327.2 2.9 copy.81
  330.1 2.9 copy.82
  333.0 3.3 add_multiply_fusion
  336.9 7.6 %copy.74 = f32[256,3,2,1024]{3,2,1,0:T(2,128)} copy(f32[256,3,2,1024]{3,0,2,1:T(8,128)S(1)} %pad_maximum_fusion.1) | data formatting | bytes 12582912 | tf_op jit(solution)/shard_map/stack | solution.py:41
  344.5 143.3 %all_to_all.33 = f32[256,3,2,1024]{3,2,1,0:T(2,128)S(1)} all-to-all(f32[256,3,2,1024]{3,2,1,0:T(2,128)} %copy.74), channel_id=1, replica_groups=mesh['gz'=8,'ky'=4] {'gz'}, dimensions={0} | all-to-all | bytes 12582912 | tf_op jit(solution)/shard_map/all_to_all | solution.py:92
  487.7 6.7 %copy.84 = f32[8,32,3,1,2,1024]{5,4,0,3,2,1:T(2,128)} copy(f32[8,32,3,1,2,1024]{5,4,3,2,1,0:T(2,128)S(1)} %bitcast.33) | data formatting | bytes 12582912 | tf_op jit(solution)/shard_map/all_to_all | solution.py:92
  (27 shorter events, 2.7 us)
Async XLA Ops:
  6.5 126.2 %copy-start = (bf16[256,256]{1,0:T(8,128)(2,1)S(1)}, bf16[256,256]{1,0:T(8,128)(2,1)}, u32[]{:S(2)}) copy-start(bf16[256,256]{1,0:T(8,128)(2,1)} %param.5) | copy-start | bytes 393220
  6.5 0.7 copy-start.4
  6.5 0.7 copy-start.5
  6.5 86.0 %all-gather.2.cloned.1.call-start = ((), (), s32[]{:S(2)}) async-start(), calls=%async_computation.2 | async-start | bytes 15728640 | tf_op jit(solution)/shard_map/all_gather | solution.py:68
  165.4 72.8 %all-to-all-start = ((bf16[8,2,98304]{2,1,0:T(2,128)(2,1)}), bf16[8,2,98304]{2,1,0:T(2,128)(2,1)S(1)}, u32[]{:S(2)}, u32[]{:S(2)}) async-start(bf16[8,2,98304]{2,1,0:T(2,128)(2,1)} %reshape.105), calls=%async_computation | async-start | bytes 6291456 | tf_op jit(solution)/shard_map/all_to_all | solution.py:82
  282.5 2.0 copy-start.3
  307.5 1.4 copy-start.2
  487.7 6.7 %copy-start.1 = (bf16[256,256]{1,0:T(8,128)(2,1)S(1)}, bf16[256,256]{1,0:T(8,128)(2,1)}, u32[]{:S(2)}) copy-start(bf16[256,256]{1,0:T(8,128)(2,1)} %param.5) | copy-start | bytes 393220
Sparse Core Ops, SparseCore 0:
  8.9 83.5 all-gather.1
where the time goes:
time: 507 us; the launch traced here: 501 us
  local copies, waits for them, and re-layouts  169 us (33%)
  waiting for transfers between devices  153 us (30%)
  blocking collectives  143 us (28%)
  between operations  13.6 us (3%)
  other arithmetic  12.1 us (2%)
  starting transfers between devices  5.47 us (1%)
  matrix products  5.2 us (1%)
    all_to_all x1, blocking collectives, per_device(): lax.all_to_all(coupled, 'gz', split_axis=0, concat_axis=3, tiled=True)  143 us
    all_gather x1, waiting for transfers between devices, per_device(): everything = lax.all_gather(fields, 'ky', axis=3, tiled=True)  84.7 us
    all_to_all x1, waiting for transfers between devices, per_device(): lax.all_to_all(walled, 'gz', split_axis=3, concat_axis=0, tiled=True)  67.3 us
    reshape x2, local copies, waits for them, and re-layouts, per_device(): source_rows = everything.reshape(local_z, 3, 2, groups * rows_dev, width_x)  34.4 us
    unnamed x17, local copies, waits for them, and re-layouts  31.4 us
    slice x3, local copies, waits for them, and re-layouts, per_device(): flipped[:half_z].astype(jnp.float32)  19.7 us
    all_to_all x1, local copies, waits for them, and re-layouts, per_device(): lax.all_to_all(walled, 'gz', split_axis=3, concat_axis=0, tiled=True)  17.7 us
    slice x1, local copies, waits for them, and re-layouts, per_device(): flipped[half_z:].astype(jnp.float32) - pencil[half_z:].astype(jnp.float32)  15.4 us
  transfers between devices with their start and end apart: 2, of which 2 were waited for; matrix products, arithmetic and copies ran while one was open for 0% of the time, Pallas kernels for 0%

commit v1 on v0

v1 whole, which is shorter than its diff:
```python
import math

import jax
import jax.numpy as jnp
import ml_dtypes
import numpy as np
from jax import lax
from jax.experimental import pallas as pl
from jax.experimental.pallas import tpu as pltpu
from jax.sharding import PartitionSpec as P

NU_COEF = 0.05
STEP_DT = 0.3
SLOT = 8
ORDER = (2, 3, 1, 0)
BF16 = jnp.bfloat16
F32 = jnp.float32


def mode_matrix(half_z):
    row = np.arange(half_z)[:, None]
    column = np.arange(half_z)[None, :]
    norm = math.sqrt(2.0 / half_z)
    step = math.pi / (2 * half_z)
    cosine = norm * np.cos(((row * (2 * column + 1)) % (4 * half_z)) * step)
    sine = norm * np.sin((((row + 1) * (2 * (half_z - 1 - column) + 1)) % (4 * half_z)) * step)
    cosine = cosine.astype(np.float32).astype(ml_dtypes.bfloat16).astype(np.float32)
    sine = sine.astype(np.float32).astype(ml_dtypes.bfloat16).astype(np.float32)
    top = np.concatenate([0.5 * cosine, 0.5 * cosine[:, ::-1]], axis=1)
    bottom = np.concatenate([0.5 * sine[:, ::-1], -0.5 * sine], axis=1)
    whole = np.concatenate([top, bottom], axis=0)
    return np.kron(whole, np.eye(2, dtype=np.float32)).astype(ml_dtypes.bfloat16)


def mode_factors(half_z):
    index = np.arange(2 * half_z)
    wave = np.where(index < half_z, index, index - half_z + 1) * (math.pi / half_z)
    pair = np.stack([np.exp(-NU_COEF * wave * wave), STEP_DT * wave]).astype(np.float32)
    return np.broadcast_to(np.repeat(pair, 2, axis=1)[:, :, None], (2, 4 * half_z, 128)).copy()


def wall_rows(fields, wall_operator, source):
    rows, width = source.shape[0], wall_operator.shape[0]
    planes = fields.shape[0]

    def body(source_ref, fields_ref, wall_ref, out_ref):
        for field in range(3):
            block = fields_ref[:, field].reshape(2 * planes, width)
            walled = jnp.dot(block, wall_ref[...], preferred_element_type=F32).astype(BF16)
            for half in range(2):
                out_ref[half, field] = walled[:, half * 128 : half * 128 + 128]

    return pl.pallas_call(
        body,
        grid_spec=pltpu.PrefetchScalarGridSpec(
            num_scalar_prefetch=1,
            grid=(rows,),
            in_specs=[
                pl.BlockSpec((planes, 3, 2, width), lambda i, source: (0, 0, 0, source[i])),
                pl.BlockSpec((width, width), lambda i, source: (0, 0)),
            ],
            out_specs=pl.BlockSpec((2, 3, 2 * planes, 128), lambda i, source: (i, 0, 0, 0)),
        ),
        out_shape=jax.ShapeDtypeStruct((2 * rows, 3, 2 * planes, 128), BF16),
        cost_estimate=pl.CostEstimate(
            flops=rows * 12 * planes * width * width, bytes_accessed=rows * 24 * planes * width, transcendentals=0
        ),
    )(source, fields, wall_operator)


def transform(pencil, matrix, factors):
    devices, units, _, depth, lanes = pencil.shape
    size = devices * depth

    def body(pencil_ref, matrix_ref, factors_ref, out_ref):
        block = jnp.concatenate([pencil_ref[:, 0, f].reshape(size, lanes) for f in range(3)], axis=1)
        modes = jnp.dot(matrix_ref[...], block, preferred_element_type=F32)
        velocity, buoyant, magnetic = (modes[:, f * lanes : f * lanes + lanes] for f in range(3))
        damping, wave = factors_ref[0], factors_ref[1]
        coupled = (
            damping * (velocity + STEP_DT * buoyant + wave * magnetic),
            damping * (buoyant - STEP_DT * velocity),
            damping * (magnetic - wave * velocity),
        )
        for f in range(3):
            out_ref[:, 0, f] = coupled[f].astype(BF16).reshape(devices, depth, lanes)

    block = pl.BlockSpec((devices, 1, 3, depth, lanes), lambda u: (0, u, 0, 0, 0))
    return pl.pallas_call(
        body,
        grid=(units,),
        in_specs=[
            block,
            pl.BlockSpec((size, size), lambda u: (0, 0)),
            pl.BlockSpec((2, size, lanes), lambda u: (0, 0, 0)),
        ],
        out_specs=block,
        out_shape=jax.ShapeDtypeStruct(pencil.shape, BF16),
        compiler_params=pltpu.CompilerParams(vmem_limit_bytes=48 * 2**20),
        cost_estimate=pl.CostEstimate(
            flops=units * 6 * size * size * lanes, bytes_accessed=units * 12 * size * lanes, transcendentals=0
        ),
    )(pencil, matrix, factors)


def place_rows(parts, chosen, places, rows_dev, width):
    depth, lanes = parts[0].shape[2], parts[0].shape[3]
    planes = depth // 2

    def body(chosen_ref, places_ref, *refs):
        out_ref = refs[-1]
        choice = chosen_ref[pl.program_id(0)]
        for c in range(len(parts)):

            @pl.when(choice == c)
            def _(part_ref=refs[c]):
                for half in range(2):
                    for field in range(3):
                        out_ref[:, field, :, half * lanes : half * lanes + lanes] = (
                            part_ref[half, field].astype(F32).reshape(planes, 2, lanes)
                        )

        @pl.when(choice < 0)
        def _():
            out_ref[...] = jnp.zeros_like(out_ref)

    def part_spec(c):
        return pl.BlockSpec((2, 3, depth, lanes), lambda r, chosen, places: (places[c, r], 0, 0, 0))

    return pl.pallas_call(
        body,
        grid_spec=pltpu.PrefetchScalarGridSpec(
            num_scalar_prefetch=2,
            grid=(rows_dev,),
            in_specs=[part_spec(c) for c in range(len(parts))],
            out_specs=pl.BlockSpec((planes, 3, 2, width), lambda r, chosen, places: (0, 0, 0, r)),
        ),
        out_shape=jax.ShapeDtypeStruct((planes, 3, 2, rows_dev * width), F32),
        cost_estimate=pl.CostEstimate(
            flops=0, bytes_accessed=rows_dev * 36 * planes * width, transcendentals=0
        ),
    )(chosen, places, *parts)


def run(rows, fields, wall_operator, remap_offset, remap_count, matrix, factors):
    gz = lax.axis_size("gz")
    group = lax.axis_index("ky")
    width = wall_operator.shape[0]
    rows_dev = fields.shape[3] // width
    chunks = (2 * SLOT, rows - 2 * SLOT)
    order = jnp.array(ORDER, jnp.int32)

    receivers = group ^ order
    counts = remap_count[group, receivers]
    offsets = remap_offset[group, receivers]
    ends = jnp.cumsum(counts)
    starts = ends - counts
    position = jnp.arange(rows, dtype=jnp.int32)
    inside = (position[None] >= starts[:, None]) & (position[None] < ends[:, None])
    source = jnp.sum(jnp.where(inside, offsets[:, None] + position[None] - starts[:, None], 0), axis=0)

    returned, first = [], 0
    for chunk in chunks:
        walled = wall_rows(fields, wall_operator, source[first : first + chunk])
        first += chunk
        pencil = lax.all_to_all(walled, "gz", split_axis=0, concat_axis=0, tiled=True)
        pencil = pencil.reshape((gz, -1) + pencil.shape[1:])
        modes = transform(pencil, matrix, factors)
        modes = modes.reshape((-1,) + modes.shape[2:])
        returned.append(lax.all_to_all(modes, "gz", split_axis=0, concat_axis=0, tiled=True))

    done = (returned[0], returned[0], jnp.concatenate(returned))
    parts = []
    for j, flip in enumerate(ORDER[:-1]):
        base = jnp.minimum(starts[j], done[j].shape[0] // 2 - SLOT)
        window = lax.dynamic_slice_in_dim(done[j], 2 * base, 2 * SLOT, axis=0)
        pairs = [(g, g ^ flip) for g in range(lax.axis_size("ky"))]
        parts.append(lax.ppermute(window, "ky", pairs))
    parts += returned

    senders = group ^ order
    got = remap_count[:, group]
    got_start = (jnp.cumsum(got) - got)[senders]
    got = got[senders]
    sent_counts = remap_count[senders[:, None], senders[:, None] ^ order[None]]
    sent_start = jnp.sum(jnp.where(jnp.tri(4, 4, -1, dtype=bool), sent_counts, 0), axis=1)
    limits = jnp.array([d.shape[0] // 2 - SLOT for d in done] + [rows], jnp.int32)
    shift = jnp.where(order == 0, sent_start, sent_start - jnp.minimum(sent_start, limits))
    row = jnp.arange(rows_dev, dtype=jnp.int32)
    from_sender = row[None] - got_start[:, None]
    held = (from_sender >= 0) & (from_sender < got[:, None])
    place = jnp.clip(from_sender, 0, got[:, None] - 1) + shift[:, None]
    own = len(ORDER) - 1
    which = jnp.arange(own + 1, dtype=jnp.int32)[:, None]
    chosen = jnp.sum(jnp.where(held, which + 1, 0), axis=0) - 1
    chosen = jnp.where((chosen == own) & (place[own] >= chunks[0]), own + 1, chosen)
    places = jnp.concatenate([
        place[:own],
        jnp.clip(place[own:], 0, chunks[0] - 1),
        jnp.clip(place[own:] - chunks[0], 0, chunks[1] - 1),
    ])
    return place_rows(parts, chosen, places, rows_dev, width)


def per_device(fields, wall_operator, remap_offset, remap_count):
    half_z = fields.shape[0] * lax.axis_size("gz") // 2
    matrix = jnp.asarray(mode_matrix(half_z))
    factors = jnp.asarray(mode_factors(half_z))
    rows_dev = fields.shape[3] // wall_operator.shape[0]
    return run(rows_dev, fields, wall_operator, remap_offset, remap_count, matrix, factors)


def solution(mesh):
    placed = (P("gz", None, None, "ky"), P(), P(), P())
    return jax.shard_map(
        per_device, mesh=mesh, in_specs=placed, out_specs=P("gz", None, None, "ky"), check_vma=False
    )
```

time: 507 us -> 244 us (0.48)
  the two profiles are of different devices: /device:TPU:17 before, /device:TPU:0 now
where the time goes in v1:
time: 244 us; the launch traced here: 243 us
  waiting for transfers between devices  161 us (66%)
  Pallas kernels  43.8 us (18%)
  starting transfers between devices  21.1 us (9%)
  local copies, waits for them, and re-layouts  10.3 us (4%)
  other arithmetic  4.62 us (2%)
    all_to_all x2, waiting for transfers between devices, run(): lax.all_to_all(modes, 'gz', split_axis=0, concat_axis=0, tiled=True)  68.4 us
    all_to_all x2, waiting for transfers between devices, run(): lax.all_to_all(walled, 'gz', split_axis=0, concat_axis=0, tiled=True)  59.5 us
    ppermute x3, waiting for transfers between devices, run(): parts.append(lax.ppermute(window, 'ky', pairs))  33.5 us
    pallas_call x2, Pallas kernels, wall_rows(): pl.pallas_call(body, grid_spec=pltpu.PrefetchScalarGridSpec(num_scalar_pr...  20.4 us
    pallas_call x1, Pallas kernels, place_rows(): pl.pallas_call(body, grid_spec=pltpu.PrefetchScalarGridSpec(num_scalar_pr...  18.3 us
    all_to_all x2, starting transfers between devices, run(): lax.all_to_all(walled, 'gz', split_axis=0, concat_axis=0, tiled=True)  10.9 us
    all_to_all x2, starting transfers between devices, run(): lax.all_to_all(modes, 'gz', split_axis=0, concat_axis=0, tiled=True)  8.06 us
    pallas_call x2, Pallas kernels, transform(): pl.pallas_call(body, grid=(units,), in_specs=[block, pl.BlockSpec((size,...  4.99 us
  transfers between devices with their start and end apart: 7, of which 6 were waited for; matrix products, arithmetic and copies ran while one was open for 1% of the time, Pallas kernels for 7%

profile of v1, /device:TPU:0, one launch (start us, length us, event | category | flops | bytes accessed | tf_op | source)
XLA Modules:
  0.0 243.2 jit_solution(10598275218630166111)
XLA Ops:
  0.0 0.7 shift-left_or_fusion
  0.7 0.9 fusion.9
  1.6 1.3 gather_fusion.3
  2.9 0.6 gather_fusion.4
  3.7 0.7 fusion.3
  4.6 0.7 gather_fusion.2
  5.5 0.6 gather_fusion.1
  6.2 0.6 gather_fusion
  7.7 9.2 %shard_map.84 = bf16[32,3,64,128]{3,2,1,0:T(8,128)(2,1)} custom-call(s32[16]{0:T(128)} %get-tuple-element.14.source_ref, bf16[32,3,2,8192]{3,2,1,0:T(2,128)(2,1)} %fields_ref.3, bf16[256,256]{1,0:T(8,128)(2,1)} %wall_ref.3), custom_call_target="tpu_custom_call" | custom-call | flops 402653184 | bytes 3145728 | tf_op jit(solution)/shard_map/pallas_call | solution.py:53
  16.9 7.3 %all-to-all-start.2 = ((bf16[32,3,64,128]{3,2,1,0:T(8,128)(2,1)}), bf16[32,3,64,128]{3,2,1,0:T(8,128)(2,1)S(1)}, u32[]{:S(2)}, u32[]{:S(2)}) async-start(bf16[32,3,64,128]{3,2,1,0:T(8,128)(2,1)} %shard_map.84), calls=%async_computation.2 | async-start | bytes 3145728 | tf_op jit(solution)/shard_map/all_to_all | solution.py:166
  24.2 11.2 %shard_map.82 = bf16[32,3,64,128]{3,2,1,0:T(8,128)(2,1)} custom-call(s32[16]{0:T(128)} %get-tuple-element.15.source_ref, bf16[32,3,2,8192]{3,2,1,0:T(2,128)(2,1)} %fields_ref.3, bf16[256,256]{1,0:T(8,128)(2,1)} %wall_ref.3), custom_call_target="tpu_custom_call" | custom-call | flops 402653184 | bytes 3145728 | tf_op jit(solution)/shard_map/pallas_call | solution.py:53
  35.4 27.4 %all-to-all-done.2 = bf16[32,3,64,128]{3,2,1,0:T(8,128)(2,1)S(1)} async-done(((bf16[32,3,64,128]{3,2,1,0:T(8,128)(2,1)}), bf16[32,3,64,128]{3,2,1,0:T(8,128)(2,1)S(1)}, u32[]{:S(2)}, u32[]{:S(2)}) %all-to-all-start.2) | async-done | bytes 1572896 | tf_op jit(solution)/shard_map/all_to_all | solution.py:166
  62.8 3.6 %all-to-all-start = ((bf16[32,3,64,128]{3,2,1,0:T(8,128)(2,1)}), bf16[32,3,64,128]{3,2,1,0:T(8,128)(2,1)S(1)}, u32[]{:S(2)}, u32[]{:S(2)}) async-start(bf16[32,3,64,128]{3,2,1,0:T(8,128)(2,1)} %shard_map.82), calls=%async_computation | async-start | bytes 3145728 | tf_op jit(solution)/shard_map/all_to_all | solution.py:166
  66.4 1.0 copy-done.2
  67.5 1.0 copy-done.4
  68.5 2.0 shard_map.85
  70.6 1.1 copy-done.1
  71.7 32.1 %all-to-all-done = bf16[32,3,64,128]{3,2,1,0:T(8,128)(2,1)S(1)} async-done(((bf16[32,3,64,128]{3,2,1,0:T(8,128)(2,1)}), bf16[32,3,64,128]{3,2,1,0:T(8,128)(2,1)S(1)}, u32[]{:S(2)}, u32[]{:S(2)}) %all-to-all-start) | async-done | bytes 1572896 | tf_op jit(solution)/shard_map/all_to_all | solution.py:166
  103.8 4.4 %all-to-all-start.3 = ((bf16[32,3,64,128]{3,2,1,0:T(8,128)(2,1)}), bf16[32,3,64,128]{3,2,1,0:T(8,128)(2,1)}, u32[]{:S(2)}, u32[]{:S(2)}) async-start(bf16[32,3,64,128]{3,2,1,0:T(8,128)(2,1)} %bitcast.19), calls=%async_computation.3 | async-start | bytes 3145728 | tf_op jit(solution)/shard_map/all_to_all | solution.py:170
  108.2 3.0 %shard_map.83 = bf16[8,4,3,64,128]{4,3,2,1,0:T(8,128)(2,1)} custom-call(bf16[8,4,3,64,128]{4,3,2,1,0:T(8,128)(2,1)S(1)} %bitcast.17, bf16[512,512]{1,0:T(8,128)(2,1)S(1)} %copy-done.5, f32[2,512,128]{2,1,0:T(8,128)S(1)} %copy-done.3), custom_call_target="tpu_custom_call" | custom-call | flops 805306368 | bytes 3145728 | tf_op jit(solution)/shard_map/pallas_call | solution.py:89
  111.2 33.6 %all-to-all-done.3.refs_4_ = bf16[32,3,64,128]{3,2,1,0:T(8,128)(2,1)} async-done(((bf16[32,3,64,128]{3,2,1,0:T(8,128)(2,1)}), bf16[32,3,64,128]{3,2,1,0:T(8,128)(2,1)}, u32[]{:S(2)}, u32[]{:S(2)}) %all-to-all-start.3) | async-done | bytes 1572896 | tf_op jit(solution)/shard_map/all_to_all | solution.py:170
  144.8 3.6 %all-to-all-start.1 = ((bf16[32,3,64,128]{3,2,1,0:T(8,128)(2,1)}), bf16[32,3,64,128]{3,2,1,0:T(8,128)(2,1)S(1)}, u32[]{:S(2)}, u32[]{:S(2)}) async-start(bf16[32,3,64,128]{3,2,1,0:T(8,128)(2,1)} %bitcast.4), calls=%async_computation.1 | async-start | bytes 3145728 | tf_op jit(solution)/shard_map/all_to_all | solution.py:170
  148.5 0.6 fusion.11
  150.9 34.8 %all-to-all-done.1.refs_3_ = bf16[32,3,64,128]{3,2,1,0:T(8,128)(2,1)S(1)} async-done(((bf16[32,3,64,128]{3,2,1,0:T(8,128)(2,1)}), bf16[32,3,64,128]{3,2,1,0:T(8,128)(2,1)S(1)}, u32[]{:S(2)}, u32[]{:S(2)}) %all-to-all-start.1) | async-done | bytes 1572896 | tf_op jit(solution)/shard_map/all_to_all | solution.py:170
  185.7 1.4 fusion
  187.2 0.7 collective-permute-start.1
  187.9 1.4 collective-permute-start
  189.4 0.6 pad_add_fusion.places_ref
  190.5 16.1 %collective-permute-done.1.refs_1_ = bf16[16,3,64,128]{3,2,1,0:T(8,128)(2,1)S(1)} collective-permute-done((bf16[16,3,64,128]{3,2,1,0:T(8,128)(2,1)S(1)}, bf16[16,3,64,128]{3,2,1,0:T(8,128)(2,1)S(1)}, u32[]{:S(2)}, u32[]{:S(2)}) %collective-permute-start.1) | collective-permute-done | bytes 786464 | tf_op jit(solution)/shard_map/ppermute | solution.py:178
  206.5 17.4 %collective-permute-done.refs_0_ = bf16[16,3,64,128]{3,2,1,0:T(8,128)(2,1)S(1)} collective-permute-done((bf16[16,3,64,128]{3,2,1,0:T(8,128)(2,1)S(1)}, bf16[16,3,64,128]{3,2,1,0:T(8,128)(2,1)S(1)}, u32[]{:S(2)}, u32[]{:S(2)}) %collective-permute-start) | collective-permute-done | bytes 786464 | tf_op jit(solution)/shard_map/ppermute | solution.py:178
  224.0 0.9 copy-done.10
  224.9 18.3 %shard_map.86 = f32[32,3,2,8192]{3,2,1,0:T(2,128)} custom-call(s32[32]{0:T(128)} %fusion.8.chosen_ref, s32[5,32]{1,0:T(8,128)} %pad_add_fusion.places_ref, bf16[16,3,64,128]{3,2,1,0:T(8,128)(2,1)} %copy-done.10, bf16[16,3,64,128]{3,2,1,0:T(8,128)(2,1)} %copy-done.9, bf16[16,3,64,128]{3,2,1,0:T(8,128)(2,1)} %copy-done.8, bf16[32,3,64,128]{3,2,1,0:T(8,128)(2,1)} %copy-done.7, ...), custom_call_target="tpu_custom_call" | custom-call | bytes 9437184 | tf_op jit(solution)/shard_map/pallas_call | solution.py:130
  (42 shorter events, 2.1 us)
Async XLA Ops:
  0.0 2.9 %copy-start = (s32[4,4]{1,0:T(4,128)S(1)}, s32[4,4]{1,0:T(4,128)}, u32[]{:S(2)}) copy-start(s32[4,4]{1,0:T(4,128)} %param.10) | copy-start | bytes 196
  0.0 4.6 %copy-start.6 = (s32[4,4]{1,0:T(4,128)S(1)}, s32[4,4]{1,0:T(4,128)}, u32[]{:S(2)}) copy-start(s32[4,4]{1,0:T(4,128)} %param.11) | copy-start | bytes 196
  4.6 2.4 copy-start.11
  4.6 2.4 copy-start.12
  16.9 45.9 %all-to-all-start.2 = ((bf16[32,3,64,128]{3,2,1,0:T(8,128)(2,1)}), bf16[32,3,64,128]{3,2,1,0:T(8,128)(2,1)S(1)}, u32[]{:S(2)}, u32[]{:S(2)}) async-start(bf16[32,3,64,128]{3,2,1,0:T(8,128)(2,1)} %shard_map.84), calls=%async_computation.2 | async-start | bytes 3145728 | tf_op jit(solution)/shard_map/all_to_all | solution.py:166
  62.8 41.0 %all-to-all-start = ((bf16[32,3,64,128]{3,2,1,0:T(8,128)(2,1)}), bf16[32,3,64,128]{3,2,1,0:T(8,128)(2,1)S(1)}, u32[]{:S(2)}, u32[]{:S(2)}) async-start(bf16[32,3,64,128]{3,2,1,0:T(8,128)(2,1)} %shard_map.82), calls=%async_computation | async-start | bytes 3145728 | tf_op jit(solution)/shard_map/all_to_all | solution.py:166
  66.4 1.0 copy-start.2
  67.5 1.0 copy-start.4
  70.5 1.2 copy-start.1
  103.8 4.4 %copy-start.3 = (f32[2,512,128]{2,1,0:T(8,128)S(1)}, f32[2,512,128]{2,1,0:T(8,128)}, u32[]{:S(2)}) copy-start(f32[2,512,128]{2,1,0:T(8,128)} %constant.60.clone.factors_ref) | copy-start | bytes 1572868
  103.8 4.4 %copy-start.5 = (bf16[512,512]{1,0:T(8,128)(2,1)S(1)}, bf16[512,512]{1,0:T(8,128)(2,1)}, u32[]{:S(2)}) copy-start(bf16[512,512]{1,0:T(8,128)(2,1)} %constant.59.clone.matrix_ref) | copy-start | bytes 1572868
  103.8 41.0 %all-to-all-start.3 = ((bf16[32,3,64,128]{3,2,1,0:T(8,128)(2,1)}), bf16[32,3,64,128]{3,2,1,0:T(8,128)(2,1)}, u32[]{:S(2)}, u32[]{:S(2)}) async-start(bf16[32,3,64,128]{3,2,1,0:T(8,128)(2,1)} %bitcast.19), calls=%async_computation.3 | async-start | bytes 3145728 | tf_op jit(solution)/shard_map/all_to_all | solution.py:170
  144.8 40.8 %all-to-all-start.1 = ((bf16[32,3,64,128]{3,2,1,0:T(8,128)(2,1)}), bf16[32,3,64,128]{3,2,1,0:T(8,128)(2,1)S(1)}, u32[]{:S(2)}, u32[]{:S(2)}) async-start(bf16[32,3,64,128]{3,2,1,0:T(8,128)(2,1)} %bitcast.4), calls=%async_computation.1 | async-start | bytes 3145728 | tf_op jit(solution)/shard_map/all_to_all | solution.py:170
  185.7 1.4 copy-start.7
  187.1 3.4 %collective-permute-start.2 = (bf16[16,3,64,128]{3,2,1,0:T(8,128)(2,1)S(1)}, bf16[16,3,64,128]{3,2,1,0:T(8,128)(2,1)S(1)}, u32[]{:S(2)}, u32[]{:S(2)}) collective-permute-start(bf16[16,3,64,128]{3,2,1,0:T(8,128)(2,1)S(1)} %get-tuple-element.9), channel_id=1, source_target_pairs={{0,1},{1,0},{2,3},{3,2},{4,5},{5,4},{6,7},{7,6},{8,9},{9,8},{10,11... | collective-permute-start | bytes 2359304 | tf_op jit(solution)/shard_map/ppermute | solution.py:178
  187.2 19.3 %collective-permute-start.1 = (bf16[16,3,64,128]{3,2,1,0:T(8,128)(2,1)S(1)}, bf16[16,3,64,128]{3,2,1,0:T(8,128)(2,1)S(1)}, u32[]{:S(2)}, u32[]{:S(2)}) collective-permute-start(bf16[16,3,64,128]{3,2,1,0:T(8,128)(2,1)S(1)} %get-tuple-element.10), channel_id=1, source_target_pairs={{0,3},{1,2},{2,1},{3,0},{4,7},{5,6},{6,5},{7,4},{8,11},{9,10},{10,... | collective-permute-start | bytes 2359304 | tf_op jit(solution)/shard_map/ppermute | solution.py:178
  187.9 36.0 %collective-permute-start = (bf16[16,3,64,128]{3,2,1,0:T(8,128)(2,1)S(1)}, bf16[16,3,64,128]{3,2,1,0:T(8,128)(2,1)S(1)}, u32[]{:S(2)}, u32[]{:S(2)}) collective-permute-start(bf16[16,3,64,128]{3,2,1,0:T(8,128)(2,1)S(1)} %get-tuple-element.11), channel_id=1, source_target_pairs={{0,2},{1,3},{2,0},{3,1},{4,6},{5,7},{6,4},{7,5},{8,10},{9,11},{10,... | collective-permute-start | bytes 2359304 | tf_op jit(solution)/shard_map/ppermute | solution.py:178
  190.5 33.5 %copy-start.8 = (bf16[16,3,64,128]{3,2,1,0:T(8,128)(2,1)}, bf16[16,3,64,128]{3,2,1,0:T(8,128)(2,1)S(1)}, u32[]{:S(2)}) copy-start(bf16[16,3,64,128]{3,2,1,0:T(8,128)(2,1)S(1)} %collective-permute-done.2.refs_2_) | copy-start | bytes 2359300
  206.5 17.4 %copy-start.9 = (bf16[16,3,64,128]{3,2,1,0:T(8,128)(2,1)}, bf16[16,3,64,128]{3,2,1,0:T(8,128)(2,1)S(1)}, u32[]{:S(2)}) copy-start(bf16[16,3,64,128]{3,2,1,0:T(8,128)(2,1)S(1)} %collective-permute-done.1.refs_1_) | copy-start | bytes 2359300
  224.0 0.9 copy-start.10

commit v2 on v1

v2 whole, which is shorter than its diff:
```python
import math

import jax
import jax.numpy as jnp
import ml_dtypes
import numpy as np
from jax import lax
from jax.experimental import pallas as pl
from jax.experimental.pallas import tpu as pltpu
from jax.sharding import PartitionSpec as P

NU_COEF = 0.05
STEP_DT = 0.3
SLOT = 8
LANES = 128
ORDER = (2, 3, 1, 0)
BF16 = jnp.bfloat16
F32 = jnp.float32
PARAMS = pltpu.CompilerParams(vmem_limit_bytes=56 * 2**20)


def mode_matrix(half_z):
    row = np.arange(half_z)[:, None]
    column = np.arange(half_z)[None, :]
    norm = math.sqrt(2.0 / half_z)
    step = math.pi / (2 * half_z)
    cosine = norm * np.cos(((row * (2 * column + 1)) % (4 * half_z)) * step)
    sine = norm * np.sin((((row + 1) * (2 * (half_z - 1 - column) + 1)) % (4 * half_z)) * step)
    cosine = cosine.astype(np.float32).astype(ml_dtypes.bfloat16).astype(np.float32)
    sine = sine.astype(np.float32).astype(ml_dtypes.bfloat16).astype(np.float32)
    top = np.concatenate([0.5 * cosine, 0.5 * cosine[:, ::-1]], axis=1)
    bottom = np.concatenate([0.5 * sine[:, ::-1], -0.5 * sine], axis=1)
    whole = np.concatenate([top, bottom], axis=0)
    return np.kron(whole, np.eye(2, dtype=np.float32)).astype(ml_dtypes.bfloat16)


def mode_factors(half_z):
    index = np.arange(2 * half_z)
    wave = np.where(index < half_z, index, index - half_z + 1) * (math.pi / half_z)
    pair = np.stack([np.exp(-NU_COEF * wave * wave), STEP_DT * wave]).astype(np.float32)
    return np.broadcast_to(np.repeat(pair, 2, axis=1)[:, :, None], (2, 4 * half_z, LANES)).copy()


def run_starts(count_ref, group):
    starts = [0]
    for flip in ORDER:
        starts.append(starts[-1] + count_ref[group, group ^ flip])
    return starts


def hbm_spec():
    return pl.BlockSpec(memory_space=pl.ANY)


def whole_spec(shape):
    return pl.BlockSpec(shape, lambda *_: (0,) * len(shape))


def wall_rows(first, rows, devices, tables, fields, wall_operator):
    width = wall_operator.shape[0]
    planes = fields.shape[0]
    depth = 2 * planes
    units = 2 * rows // devices
    pairs = max(1, units // 2) if units != 3 else 3

    def body(me_ref, offset_ref, count_ref, fields_ref, wall_ref, *refs):
        outs, held = refs[:devices], refs[devices]
        me, group = me_ref[0], me_ref[1]
        starts = run_starts(count_ref, group)

        def source(i):
            row = 0
            for j, flip in enumerate(ORDER):
                here = offset_ref[group, group ^ flip] + i - starts[j]
                row = jnp.where((i >= starts[j]) & (i < starts[j + 1]), here, row)
            return row

        for s in range(devices):
            if units % 2 == 0:
                wanted = [(first + (me ^ s) * pairs + v, None) for v in range(pairs)]
            else:
                wanted = [
                    (first + lax.shift_right_logical(unit, 1), unit & 1)
                    for unit in ((me ^ s) * units + u for u in range(units))
                ]
            for v, (i, _) in enumerate(wanted):
                column = pl.multiple_of(source(i) * width, width)
                for field in range(3):
                    at = (v * 3 + field) * depth
                    held[at : at + depth] = fields_ref[:, field, :, pl.ds(column, width)].reshape(depth, width)
            if units % 2 == 0:
                walled = jnp.dot(held[...], wall_ref[...], preferred_element_type=F32).astype(BF16)
                for v in range(pairs):
                    for field in range(3):
                        at = (v * 3 + field) * depth
                        for half in range(2):
                            outs[s][2 * v + half, field] = walled[at : at + depth, half * LANES : half * LANES + LANES]
            else:
                for u, (_, half) in enumerate(wanted):
                    wall = wall_ref[:, pl.ds(pl.multiple_of(half * LANES, LANES), LANES)]
                    block = held[u * 3 * depth : (u + 1) * 3 * depth]
                    walled = jnp.dot(block, wall, preferred_element_type=F32).astype(BF16)
                    for field in range(3):
                        outs[s][u, field] = walled[field * depth : field * depth + depth]

    shape = (units, 3, depth, LANES)
    return pl.pallas_call(
        body,
        grid_spec=pltpu.PrefetchScalarGridSpec(
            num_scalar_prefetch=3,
            grid=(1,),
            in_specs=[whole_spec(fields.shape), whole_spec(wall_operator.shape)],
            out_specs=[whole_spec(shape)] * devices,
            scratch_shapes=[pltpu.VMEM((pairs * 3 * depth, width), BF16)],
        ),
        out_shape=[jax.ShapeDtypeStruct(shape, BF16)] * devices,
        compiler_params=PARAMS,
        cost_estimate=pl.CostEstimate(
            flops=rows * 12 * planes * width * width, bytes_accessed=12 * planes * width * (rows + 32), transcendentals=0
        ),
    )(*tables, fields, wall_operator)


def transform(me, pencil, matrix, factors):
    devices = len(pencil)
    units, _, depth, lanes = pencil[0].shape
    size = devices * depth
    strip = 3 * lanes

    def body(me_ref, *refs):
        ins, matrix_ref, factors_ref = refs[:devices], refs[devices], refs[devices + 1]
        outs, (block, turned, scale) = refs[devices + 2 : 2 * devices + 2], refs[2 * devices + 2 :]
        for s in range(devices):
            at = pl.ds(pl.multiple_of((me_ref[0] ^ s) * depth, depth), depth)
            turned[s * depth : (s + 1) * depth] = matrix_ref[at]
            for k in range(2):
                scale[k, s * depth : (s + 1) * depth] = factors_ref[k, at]
            for u in range(units):
                for f in range(3):
                    block[at, u * strip + f * lanes : u * strip + f * lanes + lanes] = ins[s][u, f]
        for u in range(units):
            modes = jnp.dot(turned[...], block[:, u * strip : (u + 1) * strip], preferred_element_type=F32)
            velocity, buoyant, magnetic = (modes[:, f * lanes : f * lanes + lanes] for f in range(3))
            damping, wave = scale[0], scale[1]
            coupled = (
                damping * (velocity + STEP_DT * buoyant + wave * magnetic),
                damping * (buoyant - STEP_DT * velocity),
                damping * (magnetic - wave * velocity),
            )
            for f in range(3):
                rounded = coupled[f].astype(BF16)
                for s in range(devices):
                    outs[s][u, f] = rounded[s * depth : (s + 1) * depth]

    spec = whole_spec(pencil[0].shape)
    return pl.pallas_call(
        body,
        grid_spec=pltpu.PrefetchScalarGridSpec(
            num_scalar_prefetch=1,
            grid=(1,),
            in_specs=[spec] * devices + [whole_spec(matrix.shape), whole_spec(factors.shape)],
            out_specs=[spec] * devices,
            scratch_shapes=[
                pltpu.VMEM((size, units * strip), BF16),
                pltpu.VMEM((size, size), BF16),
                pltpu.VMEM((2, size, lanes), F32),
            ],
        ),
        out_shape=[jax.ShapeDtypeStruct(pencil[0].shape, BF16)] * devices,
        compiler_params=PARAMS,
        cost_estimate=pl.CostEstimate(
            flops=units * 6 * size * size * lanes, bytes_accessed=units * 12 * size * lanes, transcendentals=0
        ),
    )(me, *pencil, matrix, factors)


def unit_of(me, s, u, units, first):
    return 2 * first + (me ^ s) * units + u


def windows(which, me, count, chunks):
    buffers = [b for _, chunk in chunks for b in chunk]
    places = [(first, s) for first, chunk in chunks for s in range(len(chunk))]
    shape = (2 * SLOT,) + buffers[0].shape[1:]

    def body(me_ref, count_ref, *refs):
        ins, outs, sem = refs[: len(buffers)], refs[len(buffers) : -1], refs[-1]
        starts = run_starts(count_ref, me_ref[1])

        def each(act):
            for b, (first, s) in enumerate(places):
                units = ins[b].shape[0]
                for u in range(units):
                    unit = unit_of(me_ref[0], s, u, units, first)
                    for o, j in enumerate(which):
                        slot = unit - 2 * starts[j]

                        @pl.when((slot >= 0) & (unit < 2 * starts[j + 1]))
                        def _(b=b, u=u, o=o, slot=slot):
                            act(pltpu.make_async_copy(ins[b].at[u], outs[o].at[slot], sem.at[o, slot]))

        each(lambda copy: copy.start())
        each(lambda copy: copy.wait())

    return pl.pallas_call(
        body,
        grid_spec=pltpu.PrefetchScalarGridSpec(
            num_scalar_prefetch=2,
            grid=(1,),
            in_specs=[hbm_spec()] * len(buffers),
            out_specs=[hbm_spec()] * len(which),
            scratch_shapes=[pltpu.SemaphoreType.DMA((len(which), 2 * SLOT))],
        ),
        out_shape=[jax.ShapeDtypeStruct(shape, BF16)] * len(which),
        cost_estimate=pl.CostEstimate(flops=0, bytes_accessed=2**21 * len(which), transcendentals=0),
    )(me, count, *buffers)


def place_rows(me, count, received, chunks, rows_dev, width):
    devices = len(chunks[0][1])
    buffers = list(received) + [b for _, chunk in chunks for b in chunk]
    sizes = [b.shape[0] for b in buffers]
    firsts = [sum(sizes[:b]) for b in range(len(sizes) + 1)]
    blank = firsts[-1]
    depth, lanes = buffers[0].shape[2:]
    planes, step = depth // 2, 8

    def body(me_ref, count_ref, *refs):
        ins, out_ref, held, sem = refs[: len(buffers)], refs[-3], refs[-2], refs[-1]
        me, group = me_ref[0], me_ref[1]

        @pl.when(pl.program_id(0) == 0)
        def _():
            copies = [
                pltpu.make_async_copy(ins[b], held.at[pl.ds(firsts[b], sizes[b])], sem.at[b])
                for b in range(len(buffers))
            ]
            for copy in copies:
                copy.start()
            held[blank] = jnp.zeros(held.shape[1:], BF16)
            for copy in copies:
                copy.wait()

        own_start = run_starts(count_ref, group)[len(ORDER) - 1]
        ends = [0]
        for sender in range(len(ORDER)):
            ends.append(ends[-1] + count_ref[sender, group])

        def own_unit(unit):
            at = 0
            for c, (first, chunk) in enumerate(chunks):
                units = chunk[0].shape[0]
                base = firsts[len(received) + c * devices]
                inside = unit - 2 * first
                owner = lax.div(inside, units)
                spot = base + (owner ^ me) * units + inside - owner * units
                at = spot if c == 0 else jnp.where(inside >= 0, spot, at)
            return at

        planes_here = pl.ds(pl.multiple_of(pl.program_id(0) * 2 * step, 2 * step), 2 * step)
        for row in range(rows_dev):
            sender, slot = 0, row
            for g in range(1, len(ORDER)):
                later = row >= ends[g]
                sender = jnp.where(later, g, sender)
                slot = jnp.where(later, row - ends[g], slot)
            flip = sender ^ group
            window = jnp.where(flip == 1, 2, flip - 2)
            for half in range(2):
                at = jnp.where(flip == 0, own_unit(2 * (own_start + slot) + half), 2 * SLOT * window + 2 * slot + half)
                at = jnp.where(row < ends[-1], at, blank)
                for field in range(3):
                    block = held[at, field, planes_here].astype(F32).reshape(step, 2, lanes)
                    column = row * width + half * lanes
                    out_ref[:, field, :, column : column + lanes] = block

    return pl.pallas_call(
        body,
        grid_spec=pltpu.PrefetchScalarGridSpec(
            num_scalar_prefetch=2,
            grid=(planes // step,),
            in_specs=[hbm_spec()] * len(buffers),
            out_specs=pl.BlockSpec((step, 3, 2, rows_dev * width), lambda i, *_: (i, 0, 0, 0)),
            scratch_shapes=[
                pltpu.VMEM((blank + 1, 3, depth, lanes), BF16),
                pltpu.SemaphoreType.DMA((len(buffers),)),
            ],
        ),
        out_shape=jax.ShapeDtypeStruct((planes, 3, 2, rows_dev * width), F32),
        compiler_params=PARAMS,
        cost_estimate=pl.CostEstimate(
            flops=0, bytes_accessed=rows_dev * 36 * planes * width, transcendentals=0
        ),
    )(me, count, *buffers)


def exchange(buffers):
    devices = len(buffers)
    out = list(buffers)
    for s in reversed(range(1, devices)):
        out[s] = lax.ppermute(buffers[s], "gz", [(d, d ^ s) for d in range(devices)])
    return out


def run(rows, tables, fields, wall_operator, matrix, factors):
    devices, groups = lax.axis_size("gz"), lax.axis_size("ky")
    width = wall_operator.shape[0]
    rows_dev = fields.shape[3] // width
    me, _, count = tables
    chunks = []
    for first, size in ((0, 2 * SLOT), (2 * SLOT, rows - 2 * SLOT)):
        pencil = exchange(wall_rows(first, size, devices, tables, fields, wall_operator))
        chunks.append((first, exchange(transform(me, pencil, matrix, factors))))
    ready = windows((0, 1), me, count, chunks[:1]) + windows((2,), me, count, chunks)
    received = [
        lax.ppermute(window, "ky", [(g, g ^ flip) for g in range(groups)])
        for window, flip in zip(ready, ORDER)
    ]
    return place_rows(me, count, received, chunks, rows_dev, width)


def per_device(fields, wall_operator, remap_offset, remap_count):
    half_z = fields.shape[0] * lax.axis_size("gz") // 2
    matrix = jnp.asarray(mode_matrix(half_z))
    factors = jnp.asarray(mode_factors(half_z))
    rows_dev = fields.shape[3] // wall_operator.shape[0]
    me = jnp.stack([lax.axis_index("gz"), lax.axis_index("ky")]).astype(jnp.int32)
    tables = (me, remap_offset, remap_count)
    return run(rows_dev, tables, fields, wall_operator, matrix, factors)


def solution(mesh):
    placed = (P("gz", None, None, "ky"), P(), P(), P())
    return jax.shard_map(
        per_device, mesh=mesh, in_specs=placed, out_specs=P("gz", None, None, "ky"), check_vma=False
    )
```

time: 244 us -> 249 us (1.020)
  the two profiles are of different devices: /device:TPU:0 before, /device:TPU:17 now
where the time goes in v2:
time: 249 us; the launch traced here: 252 us
  waiting for transfers between devices  106 us (43%)
  Pallas kernels  88.9 us (36%)
  starting transfers between devices  54.7 us (22%)
    ppermute x28, waiting for transfers between devices, exchange(): lax.ppermute(buffers[s], 'gz', [(d, d ^ s) for d in range(devices)])  79.5 us
    pallas_call x2, Pallas kernels, windows(): pl.pallas_call(body, grid_spec=pltpu.PrefetchScalarGridSpec(num_scalar_pr...  60.7 us
    ppermute x28, starting transfers between devices, exchange(): lax.ppermute(buffers[s], 'gz', [(d, d ^ s) for d in range(devices)])  45.1 us
    ppermute x3, waiting for transfers between devices, run(): lax.ppermute(window, 'ky', [(g, g ^ flip) for g in range(groups)])  26.1 us
    pallas_call x2, Pallas kernels, transform(): pl.pallas_call(body, grid_spec=pltpu.PrefetchScalarGridSpec(num_scalar_pr...  10.1 us
    ppermute x3, starting transfers between devices, run(): lax.ppermute(window, 'ky', [(g, g ^ flip) for g in range(groups)])  9.62 us
    pallas_call x2, Pallas kernels, wall_rows(): pl.pallas_call(body, grid_spec=pltpu.PrefetchScalarGridSpec(num_scalar_pr...  9.43 us
    pallas_call x1, Pallas kernels, place_rows(): pl.pallas_call(body, grid_spec=pltpu.PrefetchScalarGridSpec(num_scalar_pr...  8.65 us
  transfers between devices with their start and end apart: 31, of which 16 were waited for; matrix products, arithmetic and copies ran while one was open for 0% of the time, Pallas kernels for 21%

profile of v2, /device:TPU:17, one launch (start us, length us, event | category | flops | bytes accessed | tf_op | source)
XLA Modules:
  0.0 252.4 jit_solution(2380607637785474960)
XLA Ops:
  0.6 4.7 %shard_map.67 = (bf16[4,3,64,128]{3,2,1,0:T(8,128)(2,1)}, bf16[4,3,64,128]{3,2,1,0:T(8,128)(2,1)}, bf16[4,3,64,128]{3,2,1,0:T(8,128)(2,1)}, bf16[4,3,64,128]{3,2...) custom-call(s32[2]{0:T(128)} %pad_add_fusion.me_ref, ...), custom_call_target="tpu_custom_call" | custom-call | flops 402653184 | bytes 4718592 | tf_op jit(solution)/shard_map/pallas_call | solution.py:107
  7.9 3.3 %collective-permute-start.20 = (bf16[4,3,64,128]{3,2,1,0:T(8,128)(2,1)}, bf16[4,3,64,128]{3,2,1,0:T(8,128)(2,1)S(1)}, u32[]{:S(2)}, u32[]{:S(2)}) collective-permute-start(bf16[4,3,64,128]{3,2,1,0:T(8,128)(2,1)} %get-tuple-element.62), channel_id=1, source_target_pairs={{0,20},{4,16},{8,28},{12,24},{16,4},{20,0},{24,12},{28,8},{1,21},{... | collective-permute-start | bytes 589832 | tf_op jit(solution)/shard_map/ppermute | solution.py:301
  11.3 4.7 %shard_map.64 = (bf16[4,3,64,128]{3,2,1,0:T(8,128)(2,1)}, bf16[4,3,64,128]{3,2,1,0:T(8,128)(2,1)}, bf16[4,3,64,128]{3,2,1,0:T(8,128)(2,1)}, bf16[4,3,64,128]{3,2...) custom-call(s32[2]{0:T(128)} %pad_add_fusion.me_ref, ...), custom_call_target="tpu_custom_call" | custom-call | flops 402653184 | bytes 4718592 | tf_op jit(solution)/shard_map/pallas_call | solution.py:107
  17.5 4.1 %collective-permute-done.18.refs_3_ = bf16[4,3,64,128]{3,2,1,0:T(8,128)(2,1)S(1)} collective-permute-done((bf16[4,3,64,128]{3,2,1,0:T(8,128)(2,1)}, bf16[4,3,64,128]{3,2,1,0:T(8,128)(2,1)S(1)}, u32[]{:S(2)}, u32[]{:S(2)}) %collective-permute-start.18) | collective-permute-done | bytes 196640 | tf_op jit(solution)/shard_map/ppermute | solution.py:301
  21.6 3.3 %collective-permute-start.1 = (bf16[4,3,64,128]{3,2,1,0:T(8,128)(2,1)}, bf16[4,3,64,128]{3,2,1,0:T(8,128)(2,1)S(1)}, u32[]{:S(2)}, u32[]{:S(2)}) collective-permute-start(bf16[4,3,64,128]{3,2,1,0:T(8,128)(2,1)} %get-tuple-element.41), channel_id=1, source_target_pairs={{0,8},{4,12},{8,0},{12,4},{16,24},{20,28},{24,16},{28,20},{1,9},{5... | collective-permute-start | bytes 589832 | tf_op jit(solution)/shard_map/ppermute | solution.py:301
  24.8 11.5 %collective-permute-start.2 = (bf16[4,3,64,128]{3,2,1,0:T(8,128)(2,1)}, bf16[4,3,64,128]{3,2,1,0:T(8,128)(2,1)S(1)}, u32[]{:S(2)}, u32[]{:S(2)}) collective-permute-start(bf16[4,3,64,128]{3,2,1,0:T(8,128)(2,1)} %get-tuple-element.42), channel_id=1, source_target_pairs={{0,12},{4,8},{8,4},{12,0},{16,28},{20,24},{24,20},{28,16},{1,13},{... | collective-permute-start | bytes 589832 | tf_op jit(solution)/shard_map/ppermute | solution.py:301
  36.3 3.1 %collective-permute-done.21.refs_6_ = bf16[4,3,64,128]{3,2,1,0:T(8,128)(2,1)S(1)} collective-permute-done((bf16[4,3,64,128]{3,2,1,0:T(8,128)(2,1)}, bf16[4,3,64,128]{3,2,1,0:T(8,128)(2,1)S(1)}, u32[]{:S(2)}, u32[]{:S(2)}) %collective-permute-start.21) | collective-permute-done | bytes 196640 | tf_op jit(solution)/shard_map/ppermute | solution.py:301
  39.5 5.5 %collective-permute-done.22.refs_7_ = bf16[4,3,64,128]{3,2,1,0:T(8,128)(2,1)S(1)} collective-permute-done((bf16[4,3,64,128]{3,2,1,0:T(8,128)(2,1)}, bf16[4,3,64,128]{3,2,1,0:T(8,128)(2,1)S(1)}, u32[]{:S(2)}, u32[]{:S(2)}) %collective-permute-start.22) | collective-permute-done | bytes 196640 | tf_op jit(solution)/shard_map/ppermute | solution.py:301
  45.1 2.2 collective-permute-start.6
  47.3 5.1 %shard_map.68 = (bf16[4,3,64,128]{3,2,1,0:T(8,128)(2,1)}, bf16[4,3,64,128]{3,2,1,0:T(8,128)(2,1)}, bf16[4,3,64,128]{3,2,1,0:T(8,128)(2,1)}, bf16[4,3,64,128]{3,2...) custom-call(s32[2]{0:T(128)} %pad_add_fusion.me_ref, ...), custom_call_target="tpu_custom_call" | custom-call | flops 805306368 | bytes 3145728 | tf_op jit(solution)/shard_map/pallas_call | solution.py:156
  52.9 4.0 %collective-permute-done.3.refs_4_ = bf16[4,3,64,128]{3,2,1,0:T(8,128)(2,1)S(1)} collective-permute-done((bf16[4,3,64,128]{3,2,1,0:T(8,128)(2,1)}, bf16[4,3,64,128]{3,2,1,0:T(8,128)(2,1)S(1)}, u32[]{:S(2)}, u32[]{:S(2)}) %collective-permute-start.3) | collective-permute-done | bytes 196640 | tf_op jit(solution)/shard_map/ppermute | solution.py:301
  56.9 2.7 %collective-permute-start.24 = (bf16[4,3,64,128]{3,2,1,0:T(8,128)(2,1)}, bf16[4,3,64,128]{3,2,1,0:T(8,128)(2,1)S(1)}, u32[]{:S(2)}, u32[]{:S(2)}) collective-permute-start(bf16[4,3,64,128]{3,2,1,0:T(8,128)(2,1)} %get-tuple-element.67), channel_id=1, source_target_pairs={{0,8},{4,12},{8,0},{12,4},{16,24},{20,28},{24,16},{28,20},{1,9},{5... | collective-permute-start | bytes 589832 | tf_op jit(solution)/shard_map/ppermute | solution.py:301
  59.9 4.8 %collective-permute-start.25 = (bf16[4,3,64,128]{3,2,1,0:T(8,128)(2,1)}, bf16[4,3,64,128]{3,2,1,0:T(8,128)(2,1)S(1)}, u32[]{:S(2)}, u32[]{:S(2)}) collective-permute-start(bf16[4,3,64,128]{3,2,1,0:T(8,128)(2,1)} %get-tuple-element.68), channel_id=1, source_target_pairs={{0,12},{4,8},{8,4},{12,0},{16,28},{20,24},{24,20},{28,16},{1,13},{... | collective-permute-start | bytes 589832 | tf_op jit(solution)/shard_map/ppermute | solution.py:301
  64.7 8.4 %collective-permute-done.5.refs_6_ = bf16[4,3,64,128]{3,2,1,0:T(8,128)(2,1)S(1)} collective-permute-done((bf16[4,3,64,128]{3,2,1,0:T(8,128)(2,1)}, bf16[4,3,64,128]{3,2,1,0:T(8,128)(2,1)S(1)}, u32[]{:S(2)}, u32[]{:S(2)}) %collective-permute-start.5) | collective-permute-done | bytes 196640 | tf_op jit(solution)/shard_map/ppermute | solution.py:301
  73.2 5.5 %collective-permute-done.6.refs_7_ = bf16[4,3,64,128]{3,2,1,0:T(8,128)(2,1)S(1)} collective-permute-done((bf16[4,3,64,128]{3,2,1,0:T(8,128)(2,1)}, bf16[4,3,64,128]{3,2,1,0:T(8,128)(2,1)S(1)}, u32[]{:S(2)}, u32[]{:S(2)}) %collective-permute-start.6) | collective-permute-done | bytes 196640 | tf_op jit(solution)/shard_map/ppermute | solution.py:301
  79.3 5.0 %shard_map.65 = (bf16[4,3,64,128]{3,2,1,0:T(8,128)(2,1)}, bf16[4,3,64,128]{3,2,1,0:T(8,128)(2,1)}, bf16[4,3,64,128]{3,2,1,0:T(8,128)(2,1)}, bf16[4,3,64,128]{3,2...) custom-call(s32[2]{0:T(128)} %pad_add_fusion.me_ref, ...), custom_call_target="tpu_custom_call" | custom-call | flops 805306368 | bytes 3145728 | tf_op jit(solution)/shard_map/pallas_call | solution.py:156
  84.5 1.7 collective-permute-start.29
  87.1 2.0 collective-permute-start.8
  89.1 5.1 %collective-permute-done.27.refs_13_.refs_16_ = bf16[4,3,64,128]{3,2,1,0:T(8,128)(2,1)S(1)} collective-permute-done((bf16[4,3,64,128]{3,2,1,0:T(8,128)(2,1)}, bf16[4,3,64,128]{3,2,1,0:T(8,128)(2,1)S(1)}, u32[]{:S(2)}, u32[]{:S(2)}) %collective-permute-start.27) | collective-permute-done | bytes 196640 | tf_op jit(solution)/shard_map/ppermute | solution.py:301
  94.2 6.4 %collective-permute-start.9 = (bf16[4,3,64,128]{3,2,1,0:T(8,128)(2,1)}, bf16[4,3,64,128]{3,2,1,0:T(8,128)(2,1)S(1)}, u32[]{:S(2)}, u32[]{:S(2)}) collective-permute-start(bf16[4,3,64,128]{3,2,1,0:T(8,128)(2,1)} %get-tuple-element.50), channel_id=1, source_target_pairs={{0,12},{4,8},{8,4},{12,0},{16,28},{20,24},{24,20},{28,16},{1,13},{... | collective-permute-start | bytes 589832 | tf_op jit(solution)/shard_map/ppermute | solution.py:301
  100.6 6.3 %collective-permute-done.28.refs_14_.refs_17_ = bf16[4,3,64,128]{3,2,1,0:T(8,128)(2,1)S(1)} collective-permute-done((bf16[4,3,64,128]{3,2,1,0:T(8,128)(2,1)}, bf16[4,3,64,128]{3,2,1,0:T(8,128)(2,1)S(1)}, u32[]{:S(2)}, u32[]{:S(2)}) %collective-permute-start.28) | collective-permute-done | bytes 196640 | tf_op jit(solution)/shard_map/ppermute | solution.py:301
  106.9 5.5 %collective-permute-done.29.refs_15_.refs_18_ = bf16[4,3,64,128]{3,2,1,0:T(8,128)(2,1)S(1)} collective-permute-done((bf16[4,3,64,128]{3,2,1,0:T(8,128)(2,1)}, bf16[4,3,64,128]{3,2,1,0:T(8,128)(2,1)S(1)}, u32[]{:S(2)}, u32[]{:S(2)}) %collective-permute-start.29) | collective-permute-done | bytes 196640 | tf_op jit(solution)/shard_map/ppermute | solution.py:301
  114.0 2.1 collective-permute-done.10.refs_4_.refs_7_
  116.1 10.7 %collective-permute-done.11.refs_5_.refs_8_ = bf16[4,3,64,128]{3,2,1,0:T(8,128)(2,1)S(1)} collective-permute-done((bf16[4,3,64,128]{3,2,1,0:T(8,128)(2,1)}, bf16[4,3,64,128]{3,2,1,0:T(8,128)(2,1)S(1)}, u32[]{:S(2)}, u32[]{:S(2)}) %collective-permute-start.11) | collective-permute-done | bytes 196640 | tf_op jit(solution)/shard_map/ppermute | solution.py:301
  126.8 13.8 %collective-permute-done.12.refs_6_.refs_9_ = bf16[4,3,64,128]{3,2,1,0:T(8,128)(2,1)S(1)} collective-permute-done((bf16[4,3,64,128]{3,2,1,0:T(8,128)(2,1)}, bf16[4,3,64,128]{3,2,1,0:T(8,128)(2,1)S(1)}, u32[]{:S(2)}, u32[]{:S(2)}) %collective-permute-start.12) | collective-permute-done | bytes 196640 | tf_op jit(solution)/shard_map/ppermute | solution.py:301
  140.6 5.1 %collective-permute-done.13.refs_7_.refs_10_ = bf16[4,3,64,128]{3,2,1,0:T(8,128)(2,1)S(1)} collective-permute-done((bf16[4,3,64,128]{3,2,1,0:T(8,128)(2,1)}, bf16[4,3,64,128]{3,2,1,0:T(8,128)(2,1)S(1)}, u32[]{:S(2)}, u32[]{:S(2)}) %collective-permute-start.13) | collective-permute-done | bytes 196640 | tf_op jit(solution)/shard_map/ppermute | solution.py:301
  146.4 22.9 %shard_map.69 = bf16[16,3,64,128]{3,2,1,0:T(8,128)(2,1)} custom-call(s32[2]{0:T(128)} %pad_add_fusion.me_ref, s32[4,4]{1,0:T(4,128)} %count_ref.9, bf16[4,3,64,128]{3,2,1,0:T(8,128)(2,1)} %get-tuple-element.47.refs_0_.refs_3_, bf16[4,3,64,128]{3,2,1,0:T(8,128)(2,1)} %copy-done, bf16[4,3,64,128]{3,2,1,0:T(8,128)(2,1)} %copy-done.1, ...), custom_call_target="tpu_custom_call" | custom-call | bytes 2097152 | tf_op jit(solution)/shard_map/pallas_call | solution.py:205
  169.4 37.8 %shard_map.66 = (bf16[16,3,64,128]{3,2,1,0:T(8,128)(2,1)}, bf16[16,3,64,128]{3,2,1,0:T(8,128)(2,1)}) custom-call(s32[2]{0:T(128)} %pad_add_fusion.me_ref, s32[4,4]{1,0:T(4,128)} %count_ref.9, bf16[4,3,64,128]{3,2,1,0:T(8,128)(2,1)} %get-tuple-element.47.refs_0_.refs_3_, bf16[4,3,64,128]{3,2,1,0:T(8,128)(2,1)} %copy-done, bf16[4,3,64,128]{3,2,1,0:T(8,128)(2,1)} %copy-done.1, ...), custom_call_target="tpu_custom_call" | custom-call | bytes 4194304 | tf_op jit(solution)/shard_map/pallas_call | solution.py:205
  207.2 9.6 %collective-permute-start.14 = (bf16[16,3,64,128]{3,2,1,0:T(8,128)(2,1)}, bf16[16,3,64,128]{3,2,1,0:T(8,128)(2,1)S(1)}, u32[]{:S(2)}, u32[]{:S(2)}) collective-permute-start(bf16[16,3,64,128]{3,2,1,0:T(8,128)(2,1)} %get-tuple-element.55), channel_id=1, source_target_pairs={{0,2},{1,3},{2,0},{3,1},{4,6},{5,7},{6,4},{7,5},{8,10},{9,11},{10,... | collective-permute-start | bytes 2359304 | tf_op jit(solution)/shard_map/ppermute | solution.py:316
  216.8 17.1 %collective-permute-done.14.refs_0_ = bf16[16,3,64,128]{3,2,1,0:T(8,128)(2,1)S(1)} collective-permute-done((bf16[16,3,64,128]{3,2,1,0:T(8,128)(2,1)}, bf16[16,3,64,128]{3,2,1,0:T(8,128)(2,1)S(1)}, u32[]{:S(2)}, u32[]{:S(2)}) %collective-permute-start.14) | collective-permute-done | bytes 786464 | tf_op jit(solution)/shard_map/ppermute | solution.py:316
  233.8 9.0 %collective-permute-done.15.refs_1_ = bf16[16,3,64,128]{3,2,1,0:T(8,128)(2,1)S(1)} collective-permute-done((bf16[16,3,64,128]{3,2,1,0:T(8,128)(2,1)}, bf16[16,3,64,128]{3,2,1,0:T(8,128)(2,1)S(1)}, u32[]{:S(2)}, u32[]{:S(2)}) %collective-permute-start.15) | collective-permute-done | bytes 786464 | tf_op jit(solution)/shard_map/ppermute | solution.py:316
  243.8 8.7 %shard_map.70 = f32[32,3,2,8192]{3,2,1,0:T(2,128)} custom-call(s32[2]{0:T(128)} %pad_add_fusion.me_ref, s32[4,4]{1,0:T(4,128)} %count_ref.9, bf16[16,3,64,128]{3,2,1,0:T(8,128)(2,1)} %copy-done.8, bf16[16,3,64,128]{3,2,1,0:T(8,128)(2,1)} %copy-done.9, bf16[16,3,64,128]{3,2,1,0:T(8,128)(2,1)} %copy-done.7, ...), custom_call_target="tpu_custom_call" | custom-call | bytes 9437184 | tf_op jit(solution)/shard_map/pallas_call | solution.py:277
  (100 shorter events, 10.4 us)
Async XLA Ops:
  5.3 10.7 %collective-permute-start.16 = (bf16[4,3,64,128]{3,2,1,0:T(8,128)(2,1)}, bf16[4,3,64,128]{3,2,1,0:T(8,128)(2,1)S(1)}, u32[]{:S(2)}, u32[]{:S(2)}) collective-permute-start(bf16[4,3,64,128]{3,2,1,0:T(8,128)(2,1)} %get-tuple-element.58), channel_id=1, source_target_pairs={{0,4},{4,0},{8,12},{12,8},{16,20},{20,16},{24,28},{28,24},{1,5},{5... | collective-permute-start | bytes 589832 | tf_op jit(solution)/shard_map/ppermute | solution.py:301
  6.5 9.7 %collective-permute-start.17 = (bf16[4,3,64,128]{3,2,1,0:T(8,128)(2,1)}, bf16[4,3,64,128]{3,2,1,0:T(8,128)(2,1)S(1)}, u32[]{:S(2)}, u32[]{:S(2)}) collective-permute-start(bf16[4,3,64,128]{3,2,1,0:T(8,128)(2,1)} %get-tuple-element.59), channel_id=1, source_target_pairs={{0,8},{4,12},{8,0},{12,4},{16,24},{20,28},{24,16},{28,20},{1,9},{5... | collective-permute-start | bytes 589832 | tf_op jit(solution)/shard_map/ppermute | solution.py:301
  7.8 13.7 %collective-permute-start.18 = (bf16[4,3,64,128]{3,2,1,0:T(8,128)(2,1)}, bf16[4,3,64,128]{3,2,1,0:T(8,128)(2,1)S(1)}, u32[]{:S(2)}, u32[]{:S(2)}) collective-permute-start(bf16[4,3,64,128]{3,2,1,0:T(8,128)(2,1)} %get-tuple-element.60), channel_id=1, source_target_pairs={{0,12},{4,8},{8,4},{12,0},{16,28},{20,24},{24,20},{28,16},{1,13},{... | collective-permute-start | bytes 589832 | tf_op jit(solution)/shard_map/ppermute | solution.py:301
  7.9 13.6 %collective-permute-start.19 = (bf16[4,3,64,128]{3,2,1,0:T(8,128)(2,1)}, bf16[4,3,64,128]{3,2,1,0:T(8,128)(2,1)S(1)}, u32[]{:S(2)}, u32[]{:S(2)}) collective-permute-start(bf16[4,3,64,128]{3,2,1,0:T(8,128)(2,1)} %get-tuple-element.61), channel_id=1, source_target_pairs={{0,16},{4,20},{8,24},{12,28},{16,0},{20,4},{24,8},{28,12},{1,17},{... | collective-permute-start | bytes 589832 | tf_op jit(solution)/shard_map/ppermute | solution.py:301
  7.9 16.9 %collective-permute-start.20 = (bf16[4,3,64,128]{3,2,1,0:T(8,128)(2,1)}, bf16[4,3,64,128]{3,2,1,0:T(8,128)(2,1)S(1)}, u32[]{:S(2)}, u32[]{:S(2)}) collective-permute-start(bf16[4,3,64,128]{3,2,1,0:T(8,128)(2,1)} %get-tuple-element.62), channel_id=1, source_target_pairs={{0,20},{4,16},{8,28},{12,24},{16,4},{20,0},{24,12},{28,8},{1,21},{... | collective-permute-start | bytes 589832 | tf_op jit(solution)/shard_map/ppermute | solution.py:301
  16.0 23.4 %collective-permute-start.21 = (bf16[4,3,64,128]{3,2,1,0:T(8,128)(2,1)}, bf16[4,3,64,128]{3,2,1,0:T(8,128)(2,1)S(1)}, u32[]{:S(2)}, u32[]{:S(2)}) collective-permute-start(bf16[4,3,64,128]{3,2,1,0:T(8,128)(2,1)} %get-tuple-element.63), channel_id=1, source_target_pairs={{0,24},{4,28},{8,16},{12,20},{16,8},{20,12},{24,0},{28,4},{1,25},{... | collective-permute-start | bytes 589832 | tf_op jit(solution)/shard_map/ppermute | solution.py:301
  16.3 28.7 %collective-permute-start.22 = (bf16[4,3,64,128]{3,2,1,0:T(8,128)(2,1)}, bf16[4,3,64,128]{3,2,1,0:T(8,128)(2,1)S(1)}, u32[]{:S(2)}, u32[]{:S(2)}) collective-permute-start(bf16[4,3,64,128]{3,2,1,0:T(8,128)(2,1)} %get-tuple-element.64), channel_id=1, source_target_pairs={{0,28},{4,24},{8,20},{12,16},{16,12},{20,8},{24,4},{28,0},{1,29},{... | collective-permute-start | bytes 589832 | tf_op jit(solution)/shard_map/ppermute | solution.py:301
  21.6 23.4 %collective-permute-start = (bf16[4,3,64,128]{3,2,1,0:T(8,128)(2,1)}, bf16[4,3,64,128]{3,2,1,0:T(8,128)(2,1)S(1)}, u32[]{:S(2)}, u32[]{:S(2)}) collective-permute-start(bf16[4,3,64,128]{3,2,1,0:T(8,128)(2,1)} %get-tuple-element.40), channel_id=1, source_target_pairs={{0,4},{4,0},{8,12},{12,8},{16,20},{20,16},{24,28},{28,24},{1,5},{5... | collective-permute-start | bytes 589832 | tf_op jit(solution)/shard_map/ppermute | solution.py:301
  21.6 23.5 %collective-permute-start.1 = (bf16[4,3,64,128]{3,2,1,0:T(8,128)(2,1)}, bf16[4,3,64,128]{3,2,1,0:T(8,128)(2,1)S(1)}, u32[]{:S(2)}, u32[]{:S(2)}) collective-permute-start(bf16[4,3,64,128]{3,2,1,0:T(8,128)(2,1)} %get-tuple-element.41), channel_id=1, source_target_pairs={{0,8},{4,12},{8,0},{12,4},{16,24},{20,28},{24,16},{28,20},{1,9},{5... | collective-permute-start | bytes 589832 | tf_op jit(solution)/shard_map/ppermute | solution.py:301
  24.8 27.6 %collective-permute-start.2 = (bf16[4,3,64,128]{3,2,1,0:T(8,128)(2,1)}, bf16[4,3,64,128]{3,2,1,0:T(8,128)(2,1)S(1)}, u32[]{:S(2)}, u32[]{:S(2)}) collective-permute-start(bf16[4,3,64,128]{3,2,1,0:T(8,128)(2,1)} %get-tuple-element.42), channel_id=1, source_target_pairs={{0,12},{4,8},{8,4},{12,0},{16,28},{20,24},{24,20},{28,16},{1,13},{... | collective-permute-start | bytes 589832 | tf_op jit(solution)/shard_map/ppermute | solution.py:301
  39.5 17.4 %collective-permute-start.3 = (bf16[4,3,64,128]{3,2,1,0:T(8,128)(2,1)}, bf16[4,3,64,128]{3,2,1,0:T(8,128)(2,1)S(1)}, u32[]{:S(2)}, u32[]{:S(2)}) collective-permute-start(bf16[4,3,64,128]{3,2,1,0:T(8,128)(2,1)} %get-tuple-element.43), channel_id=1, source_target_pairs={{0,16},{4,20},{8,24},{12,28},{16,0},{20,4},{24,8},{28,12},{1,17},{... | collective-permute-start | bytes 589832 | tf_op jit(solution)/shard_map/ppermute | solution.py:301
  45.0 14.9 %collective-permute-start.4 = (bf16[4,3,64,128]{3,2,1,0:T(8,128)(2,1)}, bf16[4,3,64,128]{3,2,1,0:T(8,128)(2,1)S(1)}, u32[]{:S(2)}, u32[]{:S(2)}) collective-permute-start(bf16[4,3,64,128]{3,2,1,0:T(8,128)(2,1)} %get-tuple-element.44), channel_id=1, source_target_pairs={{0,20},{4,16},{8,28},{12,24},{16,4},{20,0},{24,12},{28,8},{1,21},{... | collective-permute-start | bytes 589832 | tf_op jit(solution)/shard_map/ppermute | solution.py:301
  45.0 28.2 %collective-permute-start.5 = (bf16[4,3,64,128]{3,2,1,0:T(8,128)(2,1)}, bf16[4,3,64,128]{3,2,1,0:T(8,128)(2,1)S(1)}, u32[]{:S(2)}, u32[]{:S(2)}) collective-permute-start(bf16[4,3,64,128]{3,2,1,0:T(8,128)(2,1)} %get-tuple-element.45), channel_id=1, source_target_pairs={{0,24},{4,28},{8,16},{12,20},{16,8},{20,12},{24,0},{28,4},{1,25},{... | collective-permute-start | bytes 589832 | tf_op jit(solution)/shard_map/ppermute | solution.py:301
  45.1 33.6 %collective-permute-start.6 = (bf16[4,3,64,128]{3,2,1,0:T(8,128)(2,1)}, bf16[4,3,64,128]{3,2,1,0:T(8,128)(2,1)S(1)}, u32[]{:S(2)}, u32[]{:S(2)}) collective-permute-start(bf16[4,3,64,128]{3,2,1,0:T(8,128)(2,1)} %get-tuple-element.46), channel_id=1, source_target_pairs={{0,28},{4,24},{8,20},{12,16},{16,12},{20,8},{24,4},{28,0},{1,29},{... | collective-permute-start | bytes 589832 | tf_op jit(solution)/shard_map/ppermute | solution.py:301
  52.4 32.0 %collective-permute-start.23 = (bf16[4,3,64,128]{3,2,1,0:T(8,128)(2,1)}, bf16[4,3,64,128]{3,2,1,0:T(8,128)(2,1)S(1)}, u32[]{:S(2)}, u32[]{:S(2)}) collective-permute-start(bf16[4,3,64,128]{3,2,1,0:T(8,128)(2,1)} %get-tuple-element.66), channel_id=1, source_target_pairs={{0,4},{4,0},{8,12},{12,8},{16,20},{20,16},{24,28},{28,24},{1,5},{5... | collective-permute-start | bytes 589832 | tf_op jit(solution)/shard_map/ppermute | solution.py:301
  56.9 27.6 %collective-permute-start.24 = (bf16[4,3,64,128]{3,2,1,0:T(8,128)(2,1)}, bf16[4,3,64,128]{3,2,1,0:T(8,128)(2,1)S(1)}, u32[]{:S(2)}, u32[]{:S(2)}) collective-permute-start(bf16[4,3,64,128]{3,2,1,0:T(8,128)(2,1)} %get-tuple-element.67), channel_id=1, source_target_pairs={{0,8},{4,12},{8,0},{12,4},{16,24},{20,28},{24,16},{28,20},{1,9},{5... | collective-permute-start | bytes 589832 | tf_op jit(solution)/shard_map/ppermute | solution.py:301
  59.9 26.3 %collective-permute-start.25 = (bf16[4,3,64,128]{3,2,1,0:T(8,128)(2,1)}, bf16[4,3,64,128]{3,2,1,0:T(8,128)(2,1)S(1)}, u32[]{:S(2)}, u32[]{:S(2)}) collective-permute-start(bf16[4,3,64,128]{3,2,1,0:T(8,128)(2,1)} %get-tuple-element.68), channel_id=1, source_target_pairs={{0,12},{4,8},{8,4},{12,0},{16,28},{20,24},{24,20},{28,16},{1,13},{... | collective-permute-start | bytes 589832 | tf_op jit(solution)/shard_map/ppermute | solution.py:301
  73.2 14.0 %collective-permute-start.26 = (bf16[4,3,64,128]{3,2,1,0:T(8,128)(2,1)}, bf16[4,3,64,128]{3,2,1,0:T(8,128)(2,1)S(1)}, u32[]{:S(2)}, u32[]{:S(2)}) collective-permute-start(bf16[4,3,64,128]{3,2,1,0:T(8,128)(2,1)} %get-tuple-element.69), channel_id=1, source_target_pairs={{0,16},{4,20},{8,24},{12,28},{16,0},{20,4},{24,8},{28,12},{1,17},{... | collective-permute-start | bytes 589832 | tf_op jit(solution)/shard_map/ppermute | solution.py:301
  78.7 15.5 %collective-permute-start.27 = (bf16[4,3,64,128]{3,2,1,0:T(8,128)(2,1)}, bf16[4,3,64,128]{3,2,1,0:T(8,128)(2,1)S(1)}, u32[]{:S(2)}, u32[]{:S(2)}) collective-permute-start(bf16[4,3,64,128]{3,2,1,0:T(8,128)(2,1)} %get-tuple-element.70), channel_id=1, source_target_pairs={{0,20},{4,16},{8,28},{12,24},{16,4},{20,0},{24,12},{28,8},{1,21},{... | collective-permute-start | bytes 589832 | tf_op jit(solution)/shard_map/ppermute | solution.py:301
  84.4 61.4 %copy-start.10 = (bf16[4,3,64,128]{3,2,1,0:T(8,128)(2,1)}, bf16[4,3,64,128]{3,2,1,0:T(8,128)(2,1)S(1)}, u32[]{:S(2)}) copy-start(bf16[4,3,64,128]{3,2,1,0:T(8,128)(2,1)S(1)} %collective-permute-done.23.refs_9_.refs_12_) | copy-start | bytes 589828
  84.4 22.5 %collective-permute-start.28 = (bf16[4,3,64,128]{3,2,1,0:T(8,128)(2,1)}, bf16[4,3,64,128]{3,2,1,0:T(8,128)(2,1)S(1)}, u32[]{:S(2)}, u32[]{:S(2)}) collective-permute-start(bf16[4,3,64,128]{3,2,1,0:T(8,128)(2,1)} %get-tuple-element.71), channel_id=1, source_target_pairs={{0,24},{4,28},{8,16},{12,20},{16,8},{20,12},{24,0},{28,4},{1,25},{... | collective-permute-start | bytes 589832 | tf_op jit(solution)/shard_map/ppermute | solution.py:301
  84.5 27.9 %collective-permute-start.29 = (bf16[4,3,64,128]{3,2,1,0:T(8,128)(2,1)}, bf16[4,3,64,128]{3,2,1,0:T(8,128)(2,1)S(1)}, u32[]{:S(2)}, u32[]{:S(2)}) collective-permute-start(bf16[4,3,64,128]{3,2,1,0:T(8,128)(2,1)} %get-tuple-element.72), channel_id=1, source_target_pairs={{0,28},{4,24},{8,20},{12,16},{16,12},{20,8},{24,4},{28,0},{1,29},{... | collective-permute-start | bytes 589832 | tf_op jit(solution)/shard_map/ppermute | solution.py:301
  86.2 26.2 %collective-permute-start.7 = (bf16[4,3,64,128]{3,2,1,0:T(8,128)(2,1)}, bf16[4,3,64,128]{3,2,1,0:T(8,128)(2,1)S(1)}, u32[]{:S(2)}, u32[]{:S(2)}) collective-permute-start(bf16[4,3,64,128]{3,2,1,0:T(8,128)(2,1)} %get-tuple-element.48), channel_id=1, source_target_pairs={{0,4},{4,0},{8,12},{12,8},{16,20},{20,16},{24,28},{28,24},{1,5},{5... | collective-permute-start | bytes 589832 | tf_op jit(solution)/shard_map/ppermute | solution.py:301
  87.1 25.3 %collective-permute-start.8 = (bf16[4,3,64,128]{3,2,1,0:T(8,128)(2,1)}, bf16[4,3,64,128]{3,2,1,0:T(8,128)(2,1)S(1)}, u32[]{:S(2)}, u32[]{:S(2)}) collective-permute-start(bf16[4,3,64,128]{3,2,1,0:T(8,128)(2,1)} %get-tuple-element.49), channel_id=1, source_target_pairs={{0,8},{4,12},{8,0},{12,4},{16,24},{20,28},{24,16},{28,20},{1,9},{5... | collective-permute-start | bytes 589832 | tf_op jit(solution)/shard_map/ppermute | solution.py:301
  94.2 19.8 %collective-permute-start.9 = (bf16[4,3,64,128]{3,2,1,0:T(8,128)(2,1)}, bf16[4,3,64,128]{3,2,1,0:T(8,128)(2,1)S(1)}, u32[]{:S(2)}, u32[]{:S(2)}) collective-permute-start(bf16[4,3,64,128]{3,2,1,0:T(8,128)(2,1)} %get-tuple-element.50), channel_id=1, source_target_pairs={{0,12},{4,8},{8,4},{12,0},{16,28},{20,24},{24,20},{28,16},{1,13},{... | collective-permute-start | bytes 589832 | tf_op jit(solution)/shard_map/ppermute | solution.py:301
  106.9 9.2 %collective-permute-start.10 = (bf16[4,3,64,128]{3,2,1,0:T(8,128)(2,1)}, bf16[4,3,64,128]{3,2,1,0:T(8,128)(2,1)S(1)}, u32[]{:S(2)}, u32[]{:S(2)}) collective-permute-start(bf16[4,3,64,128]{3,2,1,0:T(8,128)(2,1)} %get-tuple-element.51), channel_id=1, source_target_pairs={{0,16},{4,20},{8,24},{12,28},{16,0},{20,4},{24,8},{28,12},{1,17},{... | collective-permute-start | bytes 589832 | tf_op jit(solution)/shard_map/ppermute | solution.py:301
  112.4 14.4 %collective-permute-start.11 = (bf16[4,3,64,128]{3,2,1,0:T(8,128)(2,1)}, bf16[4,3,64,128]{3,2,1,0:T(8,128)(2,1)S(1)}, u32[]{:S(2)}, u32[]{:S(2)}) collective-permute-start(bf16[4,3,64,128]{3,2,1,0:T(8,128)(2,1)} %get-tuple-element.52), channel_id=1, source_target_pairs={{0,20},{4,16},{8,28},{12,24},{16,4},{20,0},{24,12},{28,8},{1,21},{... | collective-permute-start | bytes 589832 | tf_op jit(solution)/shard_map/ppermute | solution.py:301
  112.4 28.2 %collective-permute-start.12 = (bf16[4,3,64,128]{3,2,1,0:T(8,128)(2,1)}, bf16[4,3,64,128]{3,2,1,0:T(8,128)(2,1)S(1)}, u32[]{:S(2)}, u32[]{:S(2)}) collective-permute-start(bf16[4,3,64,128]{3,2,1,0:T(8,128)(2,1)} %get-tuple-element.53), channel_id=1, source_target_pairs={{0,24},{4,28},{8,16},{12,20},{16,8},{20,12},{24,0},{28,4},{1,25},{... | collective-permute-start | bytes 589832 | tf_op jit(solution)/shard_map/ppermute | solution.py:301
  112.5 33.3 %collective-permute-start.13 = (bf16[4,3,64,128]{3,2,1,0:T(8,128)(2,1)}, bf16[4,3,64,128]{3,2,1,0:T(8,128)(2,1)S(1)}, u32[]{:S(2)}, u32[]{:S(2)}) collective-permute-start(bf16[4,3,64,128]{3,2,1,0:T(8,128)(2,1)} %get-tuple-element.54), channel_id=1, source_target_pairs={{0,28},{4,24},{8,20},{12,16},{16,12},{20,8},{24,4},{28,0},{1,29},{... | collective-permute-start | bytes 589832 | tf_op jit(solution)/shard_map/ppermute | solution.py:301
  169.3 47.5 %collective-permute-start.30 = (bf16[16,3,64,128]{3,2,1,0:T(8,128)(2,1)}, bf16[16,3,64,128]{3,2,1,0:T(8,128)(2,1)S(1)}, u32[]{:S(2)}, u32[]{:S(2)}) collective-permute-start(bf16[16,3,64,128]{3,2,1,0:T(8,128)(2,1)} %shard_map.69), channel_id=1, source_target_pairs={{0,1},{1,0},{2,3},{3,2},{4,5},{5,4},{6,7},{7,6},{8,9},{9,8},{10,11... | collective-permute-start | bytes 2359304 | tf_op jit(solution)/shard_map/ppermute | solution.py:316
  207.2 26.6 %collective-permute-start.14 = (bf16[16,3,64,128]{3,2,1,0:T(8,128)(2,1)}, bf16[16,3,64,128]{3,2,1,0:T(8,128)(2,1)S(1)}, u32[]{:S(2)}, u32[]{:S(2)}) collective-permute-start(bf16[16,3,64,128]{3,2,1,0:T(8,128)(2,1)} %get-tuple-element.55), channel_id=1, source_target_pairs={{0,2},{1,3},{2,0},{3,1},{4,6},{5,7},{6,4},{7,5},{8,10},{9,11},{10,... | collective-permute-start | bytes 2359304 | tf_op jit(solution)/shard_map/ppermute | solution.py:316
  216.8 26.1 %collective-permute-start.15 = (bf16[16,3,64,128]{3,2,1,0:T(8,128)(2,1)}, bf16[16,3,64,128]{3,2,1,0:T(8,128)(2,1)S(1)}, u32[]{:S(2)}, u32[]{:S(2)}) collective-permute-start(bf16[16,3,64,128]{3,2,1,0:T(8,128)(2,1)} %get-tuple-element.56), channel_id=1, source_target_pairs={{0,3},{1,2},{2,1},{3,0},{4,7},{5,6},{6,5},{7,4},{8,11},{9,10},{10,... | collective-permute-start | bytes 2359304 | tf_op jit(solution)/shard_map/ppermute | solution.py:316
  (30 other events, 779.7 us)
